TPU v7x, 32 devices: a whole 2x2x4 slice. The times are simulated.
32 devices in a mesh: band: 4 (over y, x), gx: 4 (over z), gy: 2 (over core).
Axes of the slice: x: 2, y: 2, z: 4, core: 2. Of those that a mesh axis runs over, the one named last changes fastest.
Arguments:
- forward: bfloat16 [4, 2, 5, 4096, 1024], P('band', None, None, 'gx', 'gy'), may hold values from -6 to 6
- adjoint: bfloat16 [4, 2, 5, 4096, 1024], P('band', None, None, 'gx', 'gy'), may hold values from -6 to 6
- freq_index: int32 [4], P('band'), may hold values from 0 to 15
- span_index: int32 [4], P('band'), may hold values from 0 to 15
Outputs:
- sensitivity: float32 [5, 4096, 1024], P(None, ('gx', 'band'), 'gy')
All inputs are finite; a program needn't handle non-finite values.
Results may differ from a plain program's by a relative error of at most 0.0003.
Values may be sent and summed in bfloat16 or wider, within the bound.
A program may use at most 128 MiB of HBM per device.

v0:
```python
import math

import jax
import jax.numpy as jnp
from jax import lax
from jax.sharding import PartitionSpec as P

FREQS = 16
SPANS = 16


def extended(block, sides, width):
    for axis, dim in sides:
        count = lax.axis_size(axis)
        forward = [(i, i + 1) for i in range(count - 1)]
        backward = [(target, source) for source, target in forward]
        low = lax.ppermute(
            lax.slice_in_dim(block, block.shape[dim] - width, None, axis=dim), axis, forward
        )
        high = lax.ppermute(lax.slice_in_dim(block, 0, width, axis=dim), axis, backward)
        block = jnp.concatenate([low, block, high], axis=dim)
    return block


def component_terms(padded_part, adjoint_part):
    centre = padded_part[2:-2, 2:-2].astype(jnp.float32)
    along_x = (
        8.0
        * (
            padded_part[3:-1, 2:-2].astype(jnp.float32)
            - padded_part[1:-3, 2:-2].astype(jnp.float32)
        )
        - (padded_part[4:, 2:-2].astype(jnp.float32) - padded_part[:-4, 2:-2].astype(jnp.float32))
    ) / 12.0
    along_y = (
        8.0
        * (
            padded_part[2:-2, 3:-1].astype(jnp.float32)
            - padded_part[2:-2, 1:-3].astype(jnp.float32)
        )
        - (padded_part[2:-2, 4:].astype(jnp.float32) - padded_part[2:-2, :-4].astype(jnp.float32))
    ) / 12.0
    adjoint_value = adjoint_part.astype(jnp.float32)
    return (adjoint_value * along_x, adjoint_value * along_y, adjoint_value, centre)


def local_terms(padded_mode, adjoint_mode, omega_m, beta_m, weight_m):
    gradient_x = 0.0
    gradient_y = 0.0
    cross = 0.0
    direct = 0.0
    for comp in range(padded_mode.shape[1]):
        gx_re, gy_re, a_re, q_re = component_terms(padded_mode[0, comp], adjoint_mode[0, comp])
        gx_im, gy_im, a_im, q_im = component_terms(padded_mode[1, comp], adjoint_mode[1, comp])
        gradient_x = gradient_x + (gx_re + gx_im)
        gradient_y = gradient_y + (gy_re + gy_im)
        cross = cross + (a_re * q_im - a_im * q_re)
        direct = direct + (a_re * q_re + a_im * q_im)
    stacked = jnp.stack([gradient_x, gradient_y, -beta_m * cross, omega_m * cross, direct])
    return weight_m * stacked


def local(forward, adjoint, freq_index, span_index):
    local_modes = forward.shape[0]
    all_modes = local_modes * lax.axis_size("band")
    omega = (freq_index.astype(jnp.float32) + 1.0) / FREQS
    beta = (span_index.astype(jnp.float32) - (SPANS - 1) / 2.0) * 2.0 / SPANS
    weight = 1.0 / (0.5 + omega)
    padded = extended(forward, (("gx", 3), ("gy", 4)), 2)
    total = local_terms(padded[0], adjoint[0], omega[0], beta[0], weight[0])
    total = total * (1.0 / math.sqrt(5.0 * all_modes))
    result = lax.psum_scatter(total, "band", scatter_dimension=1, tiled=True)
    return result


def solution(mesh):
    in_specs = (
        P("band", None, None, "gx", "gy"),
        P("band", None, None, "gx", "gy"),
        P("band"),
        P("band"),
    )
    out_specs = P(None, ("gx", "band"), "gy")
    return jax.shard_map(local, mesh=mesh, in_specs=in_specs, out_specs=out_specs, check_vma=False)
```

profile of v0, /device:TPU:0, one launch (start us, length us, event | category | flops | bytes accessed | tf_op | source)
XLA Modules:
  0.0 285.9 jit_solution(12608948772923255772)
XLA Ops:
  6.5 0.0 reduce-scatter.2.cloned.1.call-start
  6.5 1.0 fusion.44
  7.5 4.9 %collective-permute-start = (bf16[1,2,5,2,512]{4,3,2,1,0:T(2,128)(2,1)S(1)}, bf16[1,2,5,2,512]{4,3,2,1,0:T(2,128)(2,1)S(1)}, u32[]{:S(2)}, u32[]{:S(2)}) collective-permute-start(bf16[1,2,5,2,512]{4,3,2,1,0:T(2,128)(2,1)S(1)} %get-tuple-element.20), channel_id=1, source_target_pairs={{0,2},{2,4},{4,6},{1,3},{3,5},{5,7},{8,10},{10,12},{12,14},{9,11},... | collective-permute-start | bytes 61448 | tf_op jit(solution)/shard_map/ppermute | solution.py:17
  12.4 1.3 collective-permute-start.1
  13.7 14.3 %copy.12 = bf16[1,2,5,1024,512]{3,4,2,1,0:T(8,128)(2,1)} copy(bf16[1,2,5,1024,512]{4,3,2,1,0:T(8,128)(2,1)} %param.4) | data formatting | bytes 20971520 | tf_op args[0]
  28.0 0.0 collective-permute-done
  28.0 0.6 copy.11
  28.6 0.0 collective-permute-done.1
  28.6 0.6 copy.13
  29.2 21.6 %concatenate.6 = bf16[1,2,5,1028,512]{3,4,2,1,0:T(8,128)(2,1)} concatenate(bf16[1,2,5,2,512]{3,4,2,1,0:T(8,128)(2,1)S(1)} %copy.11, bf16[1,2,5,1024,512]{3,4,2,1,0:T(8,128)(2,1)} %copy.12, bf16[1,2,5,2,512]{3,4,2,1,0:T(8,128)(2,1)S(1)} %copy.13), dimensions={3} | concatenate | bytes 21053440 | tf_op jit(solution)/shard_map/concatenate | solution.py:21
  50.8 1.1 fusion.43
  51.9 1.5 collective-permute-start.2
  53.4 1.3 collective-permute-start.3
  54.7 14.2 %copy.10 = bf16[1,2,5,1024,512]{3,4,2,1,0:T(8,128)(2,1)} copy(bf16[1,2,5,1024,512]{4,3,2,1,0:T(8,128)(2,1)} %param.5) | data formatting | bytes 20971520 | tf_op args[1]
  70.2 0.0 collective-permute-done.2
  70.2 0.0 collective-permute-done.3
  70.3 0.0 slice-start
  70.3 0.0 slice-start.1
  70.3 13.0 %maximum_bitcast_fusion = bf16[2,5,1028,516]{2,3,1,0:T(8,128)(2,1)} fusion(bf16[1,2,5,1028,2]{3,4,2,1,0:T(2,128)(2,1)S(1)} %collective-permute-done.3, bf16[1,2,5,1028,512]{3,4,2,1,0:T(8,128)(2,1)} %concatenate.6, bf16[1,2,5,1028,2]{3,4,2,1,0:T(2,128)(2,1)S(1)} %collective-permute-done.2), kind=kLoop, calls=%fused_computation | loop fusion | flops 31826880 | bytes 21217920 | tf_op jit(solution)/shard_map/squeeze | solution.py:70
  83.3 0.0 slice-start.2
  83.3 5.0 %slice_bitcast_fusion.9 = (bf16[1028,516]{0,1:T(8,128)(2,1)S(1)}, bf16[1028,516]{0,1:T(8,128)(2,1)S(1)}, bf16[1028,516]{0,1:T(8,128)(2,1)S(1)}, bf16[1028,516]{0...) fusion(bf16[2,5,1028,516]{2,3,1,0:T(8,128)(2,1)} %maximum_bitca, ...), kind=kLoop, calls=%fused_computation.95 | loop fusion | bytes 21217920 | tf_op jit(solution)/shard_map/squeeze | solution.py:53
  88.3 0.0 slice-done
  88.3 0.0 slice-done.1
  88.3 0.0 slice-done.2
  88.4 17.3 %fusion.6 = f32[5,1024,512]{1,2,0:T(8,128)} fusion(bf16[1028,516]{0,1:T(8,128)(2,1)S(1)} %get-tuple-element.8, bf16[1028,516]{0,1:T(8,128)(2,1)S(1)} %get-tuple-element.9, bf16[1028,516]{0,1:T(8,128)(2,1)S(1)} %get-tuple-element.10, bf16[1028,516]{0,1:T(8,128)(2,1)S(1)} %get-tuple-element.11, bf16[1028,516]{0,1:T(8,128)(2,1)S(1)} %get-tuple-element.12, ...), kind=kLoop, calls=%fused_computation.48 | loop fusion | flops 62390272 | bytes 54525952
  105.7 27.8 %fusion.13 = f32[5,1024,512]{1,2,0:T(8,128)} fusion(f32[5,1024,512]{1,2,0:T(8,128)} %fusion.6, bf16[1028,516]{0,1:T(8,128)(2,1)S(1)} %get-tuple-element.8, bf16[1028,516]{0,1:T(8,128)(2,1)S(1)} %get-tuple-element.9, bf16[1028,516]{0,1:T(8,128)(2,1)S(1)} %get-tuple-element.10, bf16[1028,516]{0,1:T(8,128)(2,1)S(1)} %get-tuple-element.11, ...), kind=kLoop, calls=%fused_computation.55 | loop fusion | flops 62390272 | bytes 54525952
  133.5 11.7 %bitcast_dynamic-update-slice_fusion.1 = (f32[5,1024,512]{1,2,0:T(8,128)}, f32[1024,512]{0,1:T(8,128)S(1)}) fusion(f32[5,1024,512]{1,2,0:T(8,128)} %fusion.13, f32[]{:T(128)} %bitcast.35, bf16[1028,516]{0,1:T(8,128)(2,1)S(1)} %get-tuple-element.9, bf16[2,5,1024,512]{2,3,1,0:T(8,128)(2,1)S(1)} %bitcast.166, bf16[1028,516]{0,1:T(8,128)(2,1)S(1)} %get-tuple-element.8, ...), kind=kLoop, calls=%fused_computation.85 | loop fusion | flops 20971520 | bytes 25166336
  145.1 1.6 bitcast_dynamic-update-slice_fusion
  146.7 12.0 %fusion.25 = f32[5,1024,512]{1,2,0:T(8,128)} fusion(f32[5,1024,512]{1,2,0:T(8,128)} %bitcast_dynamic-update-slice_fusion, bf16[1028,516]{0,1:T(8,128)(2,1)S(1)} %get-tuple-element.9, bf16[1028,516]{0,1:T(8,128)(2,1)S(1)} %get-tuple-element.8, bf16[1028,516]{0,1:T(8,128)(2,1)S(1)} %get-tuple-element.11, bf16[1028,516]{0,1:T(8,128)(2,1)S(1)} %get-tuple-element.10, ...), kind=kLoop, calls=%fused_computation.67 | loop fusion | flops 20447232 | bytes 23068672 | tf_op jit(solution)/shard_map/stack | solution.py:59
  158.7 10.5 %multiply_multiply_fusion = f32[5,1024,512]{1,2,0:T(8,128)} fusion(f32[5,1024,512]{1,2,0:T(8,128)} %fusion.25, f32[]{:T(128)} %bitcast), kind=kLoop, calls=%fused_computation.1 | loop fusion | flops 5242880 | bytes 20971524 | tf_op jit(solution)/shard_map/mul | solution.py:71
  169.3 0.0 reduce-scatter.2.cloned.1.call-update
  169.3 106.6 %reduce-scatter.2.cloned.1.call-done = f32[5,256,512]{1,2,0:T(8,128)} async-done(((f32[5,1024,512]{1,2,0:T(8,128)}), f32[5,256,512]{1,2,0:T(8,128)}) %reduce-scatter.2.cloned.1.call-update) | async-done | bytes 2621456 | tf_op jit(solution)/shard_map/reduce_scatter | solution.py:72
  275.9 3.2 %copy.14 = f32[5,256,512]{2,1,0:T(8,128)} copy(f32[5,256,512]{1,2,0:T(8,128)} %reduce-scatter.2.cloned.1.call-done) | data formatting | bytes 5242880 | tf_op jit(solution)/shard_map/reduce_scatter | solution.py:72
  (1 shorter events, 0.0 us)
Async XLA Ops:
  6.5 269.4 %reduce-scatter.2.cloned.1.call-start = ((), (), s32[]{:S(2)}) async-start(), calls=%async_computation.1 | async-start | bytes 13107200 | tf_op jit(solution)/shard_map/reduce_scatter | solution.py:72
  7.5 20.5 %collective-permute-start = (bf16[1,2,5,2,512]{4,3,2,1,0:T(2,128)(2,1)S(1)}, bf16[1,2,5,2,512]{4,3,2,1,0:T(2,128)(2,1)S(1)}, u32[]{:S(2)}, u32[]{:S(2)}) collective-permute-start(bf16[1,2,5,2,512]{4,3,2,1,0:T(2,128)(2,1)S(1)} %get-tuple-element.20), channel_id=1, source_target_pairs={{0,2},{2,4},{4,6},{1,3},{3,5},{5,7},{8,10},{10,12},{12,14},{9,11},... | collective-permute-start | bytes 61448 | tf_op jit(solution)/shard_map/ppermute | solution.py:17
  12.4 16.2 %collective-permute-start.1 = (bf16[1,2,5,2,512]{4,3,2,1,0:T(2,128)(2,1)S(1)}, bf16[1,2,5,2,512]{4,3,2,1,0:T(2,128)(2,1)S(1)}, u32[]{:S(2)}, u32[]{:S(2)}) collective-permute-start(bf16[1,2,5,2,512]{4,3,2,1,0:T(2,128)(2,1)S(1)} %get-tuple-element.19), channel_id=1, source_target_pairs={{2,0},{4,2},{6,4},{3,1},{5,3},{7,5},{10,8},{12,10},{14,12},{11,9},... | collective-permute-start | bytes 61448 | tf_op jit(solution)/shard_map/ppermute | solution.py:20
  51.9 18.3 %collective-permute-start.2 = (bf16[1,2,5,1028,2]{3,4,2,1,0:T(2,128)(2,1)S(1)}, bf16[1,2,5,1028,2]{3,4,2,1,0:T(2,128)(2,1)S(1)}, u32[]{:S(2)}, u32[]{:S(2)}) collective-permute-start(bf16[1,2,5,1028,2]{3,4,2,1,0:T(2,128)(2,1)S(1)} %get-tuple-element.17), channel_id=1, source_target_pairs={{0,1},{2,3},{4,5},{6,7},{8,9},{10,11},{12,13},{14,15},{16,17},{18,... | collective-permute-start | bytes 123368 | tf_op jit(solution)/shard_map/ppermute | solution.py:17
  53.4 16.9 %collective-permute-start.3 = (bf16[1,2,5,1028,2]{3,4,2,1,0:T(2,128)(2,1)S(1)}, bf16[1,2,5,1028,2]{3,4,2,1,0:T(2,128)(2,1)S(1)}, u32[]{:S(2)}, u32[]{:S(2)}) collective-permute-start(bf16[1,2,5,1028,2]{3,4,2,1,0:T(2,128)(2,1)S(1)} %get-tuple-element.18), channel_id=1, source_target_pairs={{1,0},{3,2},{5,4},{7,6},{9,8},{11,10},{13,12},{15,14},{17,16},{19,... | collective-permute-start | bytes 123368 | tf_op jit(solution)/shard_map/ppermute | solution.py:20
  70.3 18.1 %slice-start = ((s8[10485760]{0:T(1024)(128)(4,1)}), s8[4194304]{0:T(1024)(128)(4,1)S(1)}, s32[]{:S(2)}) async-start(s8[10485760]{0:T(1024)(128)(4,1)} %bitcast.162), calls=%async_computation.2 | async-start | bytes 8388608
  70.3 18.1 %slice-start.1 = ((s8[10485760]{0:T(1024)(128)(4,1)}), s8[4194304]{0:T(1024)(128)(4,1)S(1)}, s32[]{:S(2)}) async-start(s8[10485760]{0:T(1024)(128)(4,1)} %bitcast.162), calls=%async_computation.3 | async-start | bytes 8388608
  83.3 5.1 %slice-start.2 = ((s8[10485760]{0:T(1024)(128)(4,1)}), s8[2097152]{0:T(1024)(128)(4,1)S(1)}, s32[]{:S(2)}) async-start(s8[10485760]{0:T(1024)(128)(4,1)} %bitcast.162), calls=%async_computation.4 | async-start | bytes 4194304
Sparse Core Ops, SparseCore 0:
  169.4 106.4 reduce-scatter.1
where the time goes:
time: 287 us; the launch traced here: 286 us
  waiting for transfers between devices  107 us (37%)
  other arithmetic  93.9 us (33%)
  local copies, waits for them, and re-layouts  61.6 us (21%)
  between operations  14.8 us (5%)
  starting transfers between devices  8.98 us (3%)
    reduce_scatter x1, waiting for transfers between devices, local(): result = lax.psum_scatter(total, 'band', scatter_dimension=1, tiled=True)  107 us
    unnamed x5, other arithmetic  58.3 us
    unnamed x8, local copies, waits for them, and re-layouts  28.5 us
    concatenate x1, local copies, waits for them, and re-layouts, extended(): block = jnp.concatenate([low, block, high], axis=dim)  21.6 us
    squeeze x1, other arithmetic, local(): total = local_terms(padded[0], adjoint[0], omega[0], beta[0], weight[0])  13 us
    another operation x1, other arithmetic, local_terms(): jnp.stack([gradient_x, gradient_y, -beta_m * cross, omega_m * cross, dire...  12 us
    mul x1, other arithmetic, local(): total = total * (1.0 / math.sqrt(5.0 * all_modes))  10.5 us
    ppermute x2, starting transfers between devices, extended(): lax.ppermute(lax.slice_in_dim(block, block.shape[dim] - width, None, axis...  6.39 us
  transfers between devices with their start and end apart: 5, of which 1 were waited for; matrix products, arithmetic and copies ran while one was open for 10% of the time, Pallas kernels for 0%

commit v1 on v0

v1 whole, which is shorter than its diff:
```python
import functools
import math

import jax
import jax.numpy as jnp
from jax import lax
from jax.experimental import pallas as pl
from jax.experimental.pallas import tpu as pltpu
from jax.sharding import PartitionSpec as P

FREQS = 16
SPANS = 16
ROWS = 128
SIDE = 16
LANES = 128
SLOTS = 3
LEVELS = 32767.0


def band_matrix(shape, offset, row_minus_column):
    row = lax.broadcasted_iota(jnp.int32, shape, 0)
    column = lax.broadcasted_iota(jnp.int32, shape, 1)
    d = (row - column if row_minus_column else column - row) - offset
    value = jnp.where(d == 1, 8.0, 0.0)
    value = jnp.where(d == -1, -8.0, value)
    value = jnp.where(d == 2, -1.0, value)
    value = jnp.where(d == -2, 1.0, value)
    return value.astype(jnp.bfloat16)


def kernel(
    bands, gxs, comps, pieces, modes,
    freq_ref, span_ref, fwd_ref, adj_ref, out_ref,
    ext, adj, acc, along_a, along_b, sent, sent_scale, got, got_scale, total, coef,
    fwd_sem, adj_sem, x_send, x_recv, y_send, y_recv,
    d_send, d_recv, s_send, s_recv, out_sem,
):
    band = lax.axis_index("band")
    gx = lax.axis_index("gx")
    gy = lax.axis_index("gy")
    nx, ny = fwd_ref.shape[1], fwd_ref.shape[2]
    others = bands - 1
    remote = others * pieces
    steps = bands * pieces
    half = 256

    def peer(k):
        if bands == 4:
            high = (band // 2 + k // 2) % 2
            return high * 2 + (band % 2 + k % 2) % 2
        return (band + k) % bands

    def place(t):
        own = t // remote
        k = (1 - own) * (others - t % others)
        piece = (1 - own) * (t // others) + own * (t - remote)
        return k, piece

    def row_of(t):
        k, piece = place(t)
        return pl.multiple_of((peer(k) * pieces + piece) * ROWS, ROWS)

    def adj_copy(t):
        slot = t % SLOTS
        return pltpu.make_async_copy(
            adj_ref.at[:, pl.ds(row_of(t), ROWS), :], adj.at[slot], adj_sem.at[slot]
        )

    fwd_copy = pltpu.make_async_copy(
        fwd_ref, ext.at[:, pl.ds(SIDE, nx), pl.ds(LANES, ny)], fwd_sem
    )
    fwd_copy.start()
    for t in range(SLOTS):
        adj_copy(t).start()

    barrier = pltpu.get_barrier_semaphore()
    for k in range(1, bands):
        target = peer(k)
        pl.semaphore_signal(barrier, inc=1, device_id={"band": target})
    pl.semaphore_signal(barrier, inc=1, device_id={"gy": 1 - gy})

    @pl.when(gx > 0)
    def _():
        pl.semaphore_signal(barrier, inc=1, device_id={"gx": gx - 1})

    @pl.when(gx < gxs - 1)
    def _():
        pl.semaphore_signal(barrier, inc=1, device_id={"gx": gx + 1})

    along_a[...] = band_matrix((ROWS, ROWS + 2 * SIDE), SIDE, False)
    along_b[...] = band_matrix((half + 2 * LANES, half), LANES, True)
    freq = jnp.full((1, ny), freq_ref[0], jnp.int32).astype(jnp.float32)
    span = jnp.full((1, ny), span_ref[0], jnp.int32).astype(jnp.float32)
    omega = (freq + 1.0) / FREQS
    beta = (span - (SPANS - 1) / 2.0) * 2.0 / SPANS
    weight = (1.0 / math.sqrt(comps * modes)) / (0.5 + omega)
    coef[0:1] = weight / 12.0
    coef[1:2] = weight / 12.0
    coef[2:3] = -beta * weight
    coef[3:4] = omega * weight
    coef[4:5] = weight

    @pl.when(gx == 0)
    def _():
        ext[:, 0:SIDE, LANES:LANES + ny] = jnp.zeros((2 * comps, SIDE, ny), jnp.bfloat16)

    @pl.when(gx == gxs - 1)
    def _():
        ext[:, SIDE + nx:, LANES:LANES + ny] = jnp.zeros((2 * comps, SIDE, ny), jnp.bfloat16)

    @pl.when(gy == 0)
    def _():
        for p in range(2 * comps):
            ext[p, SIDE:SIDE + nx, 0:LANES] = jnp.zeros((nx, LANES), jnp.bfloat16)

    @pl.when(gy == 1)
    def _():
        for p in range(2 * comps):
            ext[p, SIDE:SIDE + nx, LANES + ny:] = jnp.zeros((nx, LANES), jnp.bfloat16)

    below = (gx + gxs - 1) // gxs
    above = (2 * gxs - 2 - gx) // gxs
    pl.semaphore_wait(barrier, bands + below + above)

    def x_copy(up):
        source = nx - SIDE if up else 0
        target = 0 if up else SIDE + nx
        return pltpu.make_async_remote_copy(
            fwd_ref.at[:, pl.ds(source, SIDE), :],
            ext.at[:, pl.ds(target, SIDE), pl.ds(LANES, ny)],
            x_send.at[int(up)],
            x_recv.at[int(up)],
            device_id={"gx": gx + 1 if up else gx - 1},
        )

    def y_copy(t):
        rows = row_of(t)
        source = pl.multiple_of((1 - gy) * (ny - LANES), LANES)
        target = pl.multiple_of(gy * (LANES + ny), LANES)
        return pltpu.make_async_remote_copy(
            fwd_ref.at[:, pl.ds(rows, ROWS), pl.ds(source, LANES)],
            ext.at[:, pl.ds(rows + SIDE, ROWS), pl.ds(target, LANES)],
            y_send.at[t],
            y_recv.at[t],
            device_id={"gy": 1 - gy},
        )

    @pl.when(gx < gxs - 1)
    def _():
        x_copy(True).start()

    @pl.when(gx > 0)
    def _():
        x_copy(False).start()

    def start_y(t, carry):
        y_copy(t).start()
        return carry

    lax.fori_loop(0, steps, start_y, 0)
    fwd_copy.wait()

    @pl.when(gx > 0)
    def _():
        x_copy(True).wait_recv()

    @pl.when(gx < gxs - 1)
    def _():
        x_copy(False).wait_recv()

    def data_copy(k, piece):
        return pltpu.make_async_remote_copy(
            sent.at[k - 1, piece], got.at[k - 1, piece],
            d_send.at[k - 1, piece], d_recv.at[k - 1, piece],
            device_id={"band": peer(k)},
        )

    def scale_copy(k, piece):
        return pltpu.make_async_remote_copy(
            sent_scale.at[k - 1, piece], got_scale.at[k - 1, piece],
            s_send.at[k - 1, piece], s_recv.at[k - 1, piece],
            device_id={"band": peer(k)},
        )

    def step(t, carry):
        k, piece = place(t)
        rows = row_of(t)
        slot = t % SLOTS
        adj_copy(t).wait()
        y_copy(t).wait_recv()
        acc[...] = jnp.zeros_like(acc)

        def add_comp(comp, carry):
            for h in range(ny // half):
                cols = pl.ds(h * half, half)
                dx, dy, q, a = [], [], [], []
                for part in range(2):
                    plane = part * comps + comp
                    tall = ext[plane, pl.ds(rows, ROWS + 2 * SIDE), pl.ds(LANES + h * half, half)]
                    wide = ext[plane, pl.ds(rows + SIDE, ROWS), pl.ds(h * half, half + 2 * LANES)]
                    dx.append(jnp.dot(along_a[...], tall, preferred_element_type=jnp.float32))
                    dy.append(jnp.dot(wide, along_b[...], preferred_element_type=jnp.float32))
                    q.append(wide[:, LANES:LANES + half].astype(jnp.float32))
                    a.append(adj[slot, plane, :, cols].astype(jnp.float32))
                acc[0, :, cols] += a[0] * dx[0] + a[1] * dx[1]
                acc[1, :, cols] += a[0] * dy[0] + a[1] * dy[1]
                acc[2, :, cols] += a[0] * q[1] - a[1] * q[0]
                acc[3, :, cols] += a[0] * q[0] + a[1] * q[1]
            return carry

        lax.fori_loop(0, comps, add_comp, 0)

        @pl.when(t + SLOTS < steps)
        def _():
            adj_copy(t + SLOTS).start()

        @pl.when(t < remote)
        def _():
            for field in range(4):
                value = acc[field]
                most = jnp.maximum(jnp.max(jnp.abs(value), axis=0, keepdims=True), 1e-30)
                level = jnp.round(value * (LEVELS / most))
                sent[k - 1, piece, field] = level.astype(jnp.int32).astype(jnp.int16)
                scale = most * (1.0 / LEVELS)
                if field < 3:
                    sent_scale[k - 1, piece, field:field + 1] = scale * coef[field:field + 1]
                if field >= 2:
                    sent_scale[k - 1, piece, field + 1:field + 2] = scale * coef[field + 1:field + 2]
            data_copy(k, piece).start()
            scale_copy(k, piece).start()

        @pl.when(t >= remote)
        def _():
            for out, field in enumerate((0, 1, 2, 2, 3)):
                total[out, pl.ds(pl.multiple_of(piece * ROWS, ROWS), ROWS), :] = (
                    acc[field] * coef[out:out + 1]
                )

        return carry

    sent_scale[...] = jnp.zeros_like(sent_scale)
    lax.fori_loop(0, steps, step, 0)

    def out_copy(piece):
        rows = pl.ds(pl.multiple_of(piece * ROWS, ROWS), ROWS)
        return pltpu.make_async_copy(
            total.at[:, rows, :], out_ref.at[:, rows, :], out_sem.at[piece]
        )

    def gather(t, carry):
        k, piece = place(t)
        data_copy(k, piece).wait_recv()
        scale_copy(k, piece).wait_recv()
        rows = pl.ds(pl.multiple_of(piece * ROWS, ROWS), ROWS)
        for field in range(4):
            value = got[k - 1, piece, field].astype(jnp.int32).astype(jnp.float32)
            if field < 3:
                total[field, rows, :] += value * got_scale[k - 1, piece, field:field + 1]
            if field >= 2:
                total[field + 1, rows, :] += value * got_scale[k - 1, piece, field + 1:field + 2]

        @pl.when(t % others == others - 1)
        def _():
            out_copy(piece).start()

        return carry

    lax.fori_loop(0, remote, gather, 0)

    def finish(t, carry):
        k, piece = place(t)
        data_copy(k, piece).wait_send()
        scale_copy(k, piece).wait_send()
        return carry

    lax.fori_loop(0, remote, finish, 0)

    def finish_y(t, carry):
        y_copy(t).wait_send()
        return carry

    lax.fori_loop(0, steps, finish_y, 0)

    @pl.when(gx < gxs - 1)
    def _():
        x_copy(True).wait_send()

    @pl.when(gx > 0)
    def _():
        x_copy(False).wait_send()

    def finish_out(piece, carry):
        out_copy(piece).wait()
        return carry

    lax.fori_loop(0, pieces, finish_out, 0)


def local(bands, gxs, forward, adjoint, freq_index, span_index):
    comps, nx, ny = forward.shape[2:]
    pieces = nx // bands // ROWS
    steps = bands * pieces
    others = bands - 1
    planes = 2 * comps
    anywhere = pl.BlockSpec(memory_space=pl.ANY)
    scalar = pl.BlockSpec(memory_space=pltpu.SMEM)
    dma = pltpu.SemaphoreType.DMA
    return pl.pallas_call(
        functools.partial(kernel, bands, gxs, comps, pieces, forward.shape[0] * bands),
        out_shape=jax.ShapeDtypeStruct((5, nx // bands, ny), jnp.float32),
        in_specs=[scalar, scalar, anywhere, anywhere],
        out_specs=anywhere,
        scratch_shapes=[
            pltpu.VMEM((planes, nx + 2 * SIDE, ny + 2 * LANES), jnp.bfloat16),
            pltpu.VMEM((SLOTS, planes, ROWS, ny), jnp.bfloat16),
            pltpu.VMEM((4, ROWS, ny), jnp.float32),
            pltpu.VMEM((ROWS, ROWS + 2 * SIDE), jnp.bfloat16),
            pltpu.VMEM((256 + 2 * LANES, 256), jnp.bfloat16),
            pltpu.VMEM((others, pieces, 4, ROWS, ny), jnp.int16),
            pltpu.VMEM((others, pieces, 8, ny), jnp.float32),
            pltpu.VMEM((others, pieces, 4, ROWS, ny), jnp.int16),
            pltpu.VMEM((others, pieces, 8, ny), jnp.float32),
            pltpu.VMEM((5, nx // bands, ny), jnp.float32),
            pltpu.VMEM((8, ny), jnp.float32),
            dma(()), dma((SLOTS,)), dma((2,)), dma((2,)), dma((steps,)), dma((steps,)),
            dma((others, pieces)), dma((others, pieces)),
            dma((others, pieces)), dma((others, pieces)), dma((pieces,)),
        ],
        compiler_params=pltpu.CompilerParams(
            collective_id=0, has_side_effects=True, vmem_limit_bytes=60 * 1024 * 1024
        ),
        cost_estimate=pl.CostEstimate(
            flops=20 * planes * nx * ny, bytes_accessed=4 * planes * nx * ny, transcendentals=0
        ),
    )(
        freq_index, span_index,
        forward.reshape(planes, nx, ny), adjoint.reshape(planes, nx, ny),
    )


def solution(mesh):
    in_specs = (
        P("band", None, None, "gx", "gy"),
        P("band", None, None, "gx", "gy"),
        P("band"),
        P("band"),
    )
    out_specs = P(None, ("gx", "band"), "gy")
    body = functools.partial(local, mesh.shape["band"], mesh.shape["gx"])
    return jax.shard_map(body, mesh=mesh, in_specs=in_specs, out_specs=out_specs, check_vma=False)
```

time: 287 us -> 66.8 us (0.23)
  waiting for transfers between devices: 107 us -> 0 us
  other arithmetic: 93.9 us -> 0 us
  Pallas kernels: 0 us -> 61.7 us
  local copies, waits for them, and re-layouts: 61.6 us -> 3.62 us
  between operations: 14.8 us -> 1.3 us
  starting transfers between devices: 8.98 us -> 0 us
    reduce_scatter x1 -> x0, waiting for transfers between devices: 107 us -> none  [local(): result = lax.psum_scatter(total, 'band', scatter_dimension=1, tiled=True)]
    pallas_call x0 -> x1, Pallas kernels: none -> 61.7 us  [local(): pl.pallas_call(functools.partial(kernel, bands, gxs, comps, pieces, forwa...]
    unnamed x5 -> x0, other arithmetic: 58.3 us -> none
    unnamed x8 -> x1, local copies, waits for them, and re-layouts: 28.5 us -> 3.62 us
    concatenate x1 -> x0, local copies, waits for them, and re-layouts: 21.6 us -> none  [extended(): block = jnp.concatenate([low, block, high], axis=dim)]
    squeeze x1 -> x0, other arithmetic: 13 us -> none  [local(): total = local_terms(padded[0], adjoint[0], omega[0], beta[0], weight[0])]
    another operation x1 -> x0, other arithmetic: 12 us -> none  [local_terms(): jnp.stack([gradient_x, gradient_y, -beta_m * cross, omega_m * cross, dire...]
    mul x1 -> x0, other arithmetic: 10.5 us -> none  [local(): total = total * (1.0 / math.sqrt(5.0 * all_modes))]
  transfers between devices with their start and end apart: 5 -> 0, of which waited for: 1 -> 0; matrix products, arithmetic and copies ran while one was open for 10% -> 0% of each run, Pallas kernels for 0% -> 0%
where the time goes in v1:
time: 66.8 us; the launch traced here: 66.6 us
  Pallas kernels  61.7 us (92%)
  local copies, waits for them, and re-layouts  3.62 us (5%)
  between operations  1.3 us (2%)
    pallas_call x1, Pallas kernels, local(): pl.pallas_call(functools.partial(kernel, bands, gxs, comps, pieces, forwa...  61.7 us
    unnamed x1, local copies, waits for them, and re-layouts  3.62 us

profile of v1, /device:TPU:0, one launch (start us, length us, event | category | flops | bytes accessed | tf_op | source)
XLA Modules:
  0.0 66.6 jit_solution(12645020414992448678)
XLA Ops:
  1.3 61.7 %shard_map.46 = f32[5,256,512]{2,1,0:T(8,128)} custom-call(s32[1]{0:T(128)S(6)} %copy.6.freq_ref, s32[1]{0:T(128)S(6)} %copy.7.span_ref, bf16[10,1024,512]{2,1,0:T(8,128)(2,1)} %bitcast.2, bf16[10,1024,512]{2,1,0:T(8,128)(2,1)} %bitcast.3), custom_call_target="tpu_custom_call" | custom-call | flops 104857600 | bytes 20971520 | tf_op jit(solution)/shard_map/pallas_call | solution.py:308
  63.0 3.6 %copy.8 = f32[5,256,512]{2,1,0:T(8,128)} copy(f32[5,256,512]{2,1,0:T(8,128)} %shard_map.46) | data formatting | bytes 5242880

commit v2 on v1

--- a/solution.py
+++ b/solution.py
@@ -31,30 +31,31 @@
 def kernel(
     bands, gxs, comps, pieces, modes,
     freq_ref, span_ref, fwd_ref, adj_ref, out_ref,
-    ext, adj, acc, along_a, along_b, sent, sent_scale, got, got_scale, total, coef,
-    fwd_sem, adj_sem, x_send, x_recv, y_send, y_recv,
+    ext, adj, acc, along_a, along_b, sent, sent_sum, sent_scale,
+    got, got_sum, got_scale, total, coef,
+    joint_sem, strip_sem, adj_sem, x_send, x_recv, y_send, y_recv,
     d_send, d_recv, s_send, s_recv, out_sem,
 ):
     band = lax.axis_index("band")
     gx = lax.axis_index("gx")
     gy = lax.axis_index("gy")
     nx, ny = fwd_ref.shape[1], fwd_ref.shape[2]
-    others = bands - 1
-    remote = others * pieces
     steps = bands * pieces
+    quarter = nx // bands
     half = 256
 
     def peer(k):
-        if bands == 4:
-            high = (band // 2 + k // 2) % 2
-            return high * 2 + (band % 2 + k % 2) % 2
-        return (band + k) % bands
+        high = (band // 2 + k // 2) % 2
+        return high * 2 + (band % 2 + k % 2) % 2
 
     def place(t):
-        own = t // remote
-        k = (1 - own) * (others - t % others)
-        piece = (1 - own) * (t // others) + own * (t - remote)
-        return k, piece
+        phase, piece = t // pieces, t % pieces
+        odd = piece % 2
+        last = phase // 3
+        third = phase // 2 - last
+        first = (3 - phase) // 3
+        second = 1 - first - third - last
+        return 3 * first + (1 + odd) * second + (2 - odd) * third, piece
 
     def row_of(t):
         k, piece = place(t)
@@ -66,12 +67,27 @@
             adj_ref.at[:, pl.ds(row_of(t), ROWS), :], adj.at[slot], adj_sem.at[slot]
         )
 
-    fwd_copy = pltpu.make_async_copy(
-        fwd_ref, ext.at[:, pl.ds(SIDE, nx), pl.ds(LANES, ny)], fwd_sem
-    )
-    fwd_copy.start()
-    for t in range(SLOTS):
-        adj_copy(t).start()
+    def joint_copy(edge):
+        low, high = max(edge * quarter - SIDE, 0), min(edge * quarter + SIDE, nx)
+        return pltpu.make_async_copy(
+            fwd_ref.at[:, pl.ds(low, high - low), :],
+            ext.at[:, pl.ds(SIDE + low, high - low), pl.ds(LANES, ny)],
+            joint_sem.at[edge],
+        )
+
+    def strip_copy(k):
+        low = pl.multiple_of(peer(k) * quarter + SIDE, SIDE)
+        rows = quarter - 2 * SIDE
+        return pltpu.make_async_copy(
+            fwd_ref.at[:, pl.ds(low, rows), :],
+            ext.at[:, pl.ds(low + SIDE, rows), pl.ds(LANES, ny)],
+            strip_sem.at[k],
+        )
+
+    for edge in range(bands + 1):
+        joint_copy(edge).start()
+    strip_copy(3).start()
+    adj_copy(0).start()
 
     barrier = pltpu.get_barrier_semaphore()
     for k in range(1, bands):
@@ -157,8 +173,15 @@
         y_copy(t).start()
         return carry
 
-    lax.fori_loop(0, steps, start_y, 0)
-    fwd_copy.wait()
+    lax.fori_loop(0, pieces, start_y, 0)
+    for edge in range(bands + 1):
+        joint_copy(edge).wait()
+    strip_copy(3).wait()
+    for t in range(1, SLOTS):
+        adj_copy(t).start()
+    for k in (1, 2, 0):
+        strip_copy(k).start()
+    lax.fori_loop(pieces, steps, start_y, 0)
 
     @pl.when(gx > 0)
     def _():
@@ -168,24 +191,50 @@
     def _():
         x_copy(False).wait_recv()
 
-    def data_copy(k, piece):
+    def data_copy(phase, piece):
         return pltpu.make_async_remote_copy(
-            sent.at[k - 1, piece], got.at[k - 1, piece],
-            d_send.at[k - 1, piece], d_recv.at[k - 1, piece],
-            device_id={"band": peer(k)},
-        )
-
-    def scale_copy(k, piece):
+            sent.at[phase, piece], got.at[phase, piece],
+            d_send.at[phase, piece], d_recv.at[phase, piece],
+            device_id={"band": peer(1 + piece % 2)},
+        )
+
+    def sum_copy(piece):
         return pltpu.make_async_remote_copy(
-            sent_scale.at[k - 1, piece], got_scale.at[k - 1, piece],
-            s_send.at[k - 1, piece], s_recv.at[k - 1, piece],
-            device_id={"band": peer(k)},
-        )
+            sent_sum.at[piece], got_sum.at[piece],
+            d_send.at[2, piece], d_recv.at[2, piece],
+            device_id={"band": peer(2 - piece % 2)},
+        )
+
+    def scale_copy(phase, piece):
+        odd = piece % 2
+        third = phase // 2
+        return pltpu.make_async_remote_copy(
+            sent_scale.at[phase, piece], got_scale.at[phase, piece],
+            s_send.at[phase, piece], s_recv.at[phase, piece],
+            device_id={"band": peer((1 + odd) * (1 - third) + (2 - odd) * third)},
+        )
+
+    fields = (0, 1, 2, 2, 3)
+
+    def coded(value):
+        most = jnp.maximum(jnp.max(jnp.abs(value), axis=0, keepdims=True), 1e-30)
+        level = jnp.round(value * (LEVELS / most))
+        return level.astype(jnp.int32).astype(jnp.int16), most * (1.0 / LEVELS)
 
     def step(t, carry):
-        k, piece = place(t)
+        phase, piece = t // pieces, t % pieces
         rows = row_of(t)
         slot = t % SLOTS
+
+        @pl.when(t == pieces)
+        def _():
+            strip_copy(1).wait()
+            strip_copy(2).wait()
+
+        @pl.when(t == 3 * pieces)
+        def _():
+            strip_copy(0).wait()
+
         adj_copy(t).wait()
         y_copy(t).wait_recv()
         acc[...] = jnp.zeros_like(acc)
@@ -214,24 +263,33 @@
         def _():
             adj_copy(t + SLOTS).start()
 
-        @pl.when(t < remote)
+        @pl.when(phase < 2)
         def _():
             for field in range(4):
-                value = acc[field]
-                most = jnp.maximum(jnp.max(jnp.abs(value), axis=0, keepdims=True), 1e-30)
-                level = jnp.round(value * (LEVELS / most))
-                sent[k - 1, piece, field] = level.astype(jnp.int32).astype(jnp.int16)
-                scale = most * (1.0 / LEVELS)
-                if field < 3:
-                    sent_scale[k - 1, piece, field:field + 1] = scale * coef[field:field + 1]
-                if field >= 2:
-                    sent_scale[k - 1, piece, field + 1:field + 2] = scale * coef[field + 1:field + 2]
-            data_copy(k, piece).start()
-            scale_copy(k, piece).start()
-
-        @pl.when(t >= remote)
-        def _():
-            for out, field in enumerate((0, 1, 2, 2, 3)):
+                level, scale = coded(acc[field])
+                sent[phase, piece, field] = level
+                for out in range(5):
+                    if fields[out] == field:
+                        sent_scale[phase, piece, out:out + 1] = scale * coef[out:out + 1]
+            data_copy(phase, piece).start()
+            scale_copy(phase, piece).start()
+
+        @pl.when(phase == 2)
+        def _():
+            data_copy(0, piece).wait_recv()
+            scale_copy(0, piece).wait_recv()
+            for out, field in enumerate(fields):
+                other = got[0, piece, field].astype(jnp.int32).astype(jnp.float32)
+                value = acc[field] * coef[out:out + 1] + other * got_scale[0, piece, out:out + 1]
+                level, scale = coded(value)
+                sent_sum[piece, out] = level
+                sent_scale[2, piece, out:out + 1] = scale
+            sum_copy(piece).start()
+            scale_copy(2, piece).start()
+
+        @pl.when(phase == 3)
+        def _():
+            for out, field in enumerate(fields):
                 total[out, pl.ds(pl.multiple_of(piece * ROWS, ROWS), ROWS), :] = (
                     acc[field] * coef[out:out + 1]
                 )
@@ -247,33 +305,38 @@
             total.at[:, rows, :], out_ref.at[:, rows, :], out_sem.at[piece]
         )
 
-    def gather(t, carry):
-        k, piece = place(t)
-        data_copy(k, piece).wait_recv()
-        scale_copy(k, piece).wait_recv()
+    def add_one(piece, carry):
+        data_copy(1, piece).wait_recv()
+        scale_copy(1, piece).wait_recv()
         rows = pl.ds(pl.multiple_of(piece * ROWS, ROWS), ROWS)
-        for field in range(4):
-            value = got[k - 1, piece, field].astype(jnp.int32).astype(jnp.float32)
-            if field < 3:
-                total[field, rows, :] += value * got_scale[k - 1, piece, field:field + 1]
-            if field >= 2:
-                total[field + 1, rows, :] += value * got_scale[k - 1, piece, field + 1:field + 2]
-
-        @pl.when(t % others == others - 1)
-        def _():
-            out_copy(piece).start()
-
-        return carry
-
-    lax.fori_loop(0, remote, gather, 0)
-
-    def finish(t, carry):
-        k, piece = place(t)
-        data_copy(k, piece).wait_send()
-        scale_copy(k, piece).wait_send()
-        return carry
-
-    lax.fori_loop(0, remote, finish, 0)
+        for out, field in enumerate(fields):
+            value = got[1, piece, field].astype(jnp.int32).astype(jnp.float32)
+            total[out, rows, :] += value * got_scale[1, piece, out:out + 1]
+        return carry
+
+    lax.fori_loop(0, pieces, add_one, 0)
+
+    def add_sum(piece, carry):
+        sum_copy(piece).wait_recv()
+        scale_copy(2, piece).wait_recv()
+        rows = pl.ds(pl.multiple_of(piece * ROWS, ROWS), ROWS)
+        for out in range(5):
+            value = got_sum[piece, out].astype(jnp.int32).astype(jnp.float32)
+            total[out, rows, :] += value * got_scale[2, piece, out:out + 1]
+        out_copy(piece).start()
+        return carry
+
+    lax.fori_loop(0, pieces, add_sum, 0)
+
+    def finish(piece, carry):
+        for phase in range(2):
+            data_copy(phase, piece).wait_send()
+        sum_copy(piece).wait_send()
+        for phase in range(3):
+            scale_copy(phase, piece).wait_send()
+        return carry
+
+    lax.fori_loop(0, pieces, finish, 0)
 
     def finish_y(t, carry):
         y_copy(t).wait_send()
@@ -300,7 +363,6 @@
     comps, nx, ny = forward.shape[2:]
     pieces = nx // bands // ROWS
     steps = bands * pieces
-    others = bands - 1
     planes = 2 * comps
     anywhere = pl.BlockSpec(memory_space=pl.ANY)
     scalar = pl.BlockSpec(memory_space=pltpu.SMEM)
@@ -316,15 +378,17 @@
             pltpu.VMEM((4, ROWS, ny), jnp.float32),
             pltpu.VMEM((ROWS, ROWS + 2 * SIDE), jnp.bfloat16),
             pltpu.VMEM((256 + 2 * LANES, 256), jnp.bfloat16),
-            pltpu.VMEM((others, pieces, 4, ROWS, ny), jnp.int16),
-            pltpu.VMEM((others, pieces, 8, ny), jnp.float32),
-            pltpu.VMEM((others, pieces, 4, ROWS, ny), jnp.int16),
-            pltpu.VMEM((others, pieces, 8, ny), jnp.float32),
+            pltpu.VMEM((2, pieces, 4, ROWS, ny), jnp.int16),
+            pltpu.VMEM((pieces, 5, ROWS, ny), jnp.int16),
+            pltpu.VMEM((3, pieces, 8, ny), jnp.float32),
+            pltpu.VMEM((2, pieces, 4, ROWS, ny), jnp.int16),
+            pltpu.VMEM((pieces, 5, ROWS, ny), jnp.int16),
+            pltpu.VMEM((3, pieces, 8, ny), jnp.float32),
             pltpu.VMEM((5, nx // bands, ny), jnp.float32),
             pltpu.VMEM((8, ny), jnp.float32),
-            dma(()), dma((SLOTS,)), dma((2,)), dma((2,)), dma((steps,)), dma((steps,)),
-            dma((others, pieces)), dma((others, pieces)),
-            dma((others, pieces)), dma((others, pieces)), dma((pieces,)),
+            dma((bands + 1,)), dma((bands,)), dma((SLOTS,)), dma((2,)), dma((2,)), dma((steps,)), dma((steps,)),
+            dma((3, pieces)), dma((3, pieces)),
+            dma((3, pieces)), dma((3, pieces)), dma((pieces,)),
         ],
         compiler_params=pltpu.CompilerParams(
             collective_id=0, has_side_effects=True, vmem_limit_bytes=60 * 1024 * 1024

time: 66.8 us -> 60 us (0.90)
  Pallas kernels: 61.7 us -> 54.9 us
    pallas_call x1, Pallas kernels: 61.7 us -> 54.9 us  [local(): pl.pallas_call(functools.partial(kernel, bands, gxs, comps, pieces, forwa...]
where the time goes in v2:
time: 60 us; the launch traced here: 59.8 us
  Pallas kernels  54.9 us (92%)
  local copies, waits for them, and re-layouts  3.62 us (6%)
  between operations  1.3 us (2%)
    pallas_call x1, Pallas kernels, local(): pl.pallas_call(functools.partial(kernel, bands, gxs, comps, pieces, forwa...  54.9 us
    unnamed x1, local copies, waits for them, and re-layouts  3.62 us

profile of v2, /device:TPU:0, one launch (start us, length us, event | category | flops | bytes accessed | tf_op | source)
XLA Modules:
  0.0 59.8 jit_solution(14305569011224114123)
XLA Ops:
  1.3 54.9 %shard_map.46 = f32[5,256,512]{2,1,0:T(8,128)} custom-call(s32[1]{0:T(128)S(6)} %copy.6.freq_ref, s32[1]{0:T(128)S(6)} %copy.7.span_ref, bf16[10,1024,512]{2,1,0:T(8,128)(2,1)} %bitcast.2, bf16[10,1024,512]{2,1,0:T(8,128)(2,1)} %bitcast.3), custom_call_target="tpu_custom_call" | custom-call | flops 104857600 | bytes 20971520 | tf_op jit(solution)/shard_map/pallas_call | solution.py:370
  56.2 3.6 %copy.8 = f32[5,256,512]{2,1,0:T(8,128)} copy(f32[5,256,512]{2,1,0:T(8,128)} %shard_map.46) | data formatting | bytes 5242880

commit v3 on v2

--- a/solution.py
+++ b/solution.py
@@ -29,7 +29,7 @@
 
 
 def kernel(
-    bands, gxs, comps, pieces, modes,
+    bands, gxs, comps, pieces,
     freq_ref, span_ref, fwd_ref, adj_ref, out_ref,
     ext, adj, acc, along_a, along_b, sent, sent_sum, sent_scale,
     got, got_sum, got_scale, total, coef,
@@ -103,37 +103,6 @@
     def _():
         pl.semaphore_signal(barrier, inc=1, device_id={"gx": gx + 1})
 
-    along_a[...] = band_matrix((ROWS, ROWS + 2 * SIDE), SIDE, False)
-    along_b[...] = band_matrix((half + 2 * LANES, half), LANES, True)
-    freq = jnp.full((1, ny), freq_ref[0], jnp.int32).astype(jnp.float32)
-    span = jnp.full((1, ny), span_ref[0], jnp.int32).astype(jnp.float32)
-    omega = (freq + 1.0) / FREQS
-    beta = (span - (SPANS - 1) / 2.0) * 2.0 / SPANS
-    weight = (1.0 / math.sqrt(comps * modes)) / (0.5 + omega)
-    coef[0:1] = weight / 12.0
-    coef[1:2] = weight / 12.0
-    coef[2:3] = -beta * weight
-    coef[3:4] = omega * weight
-    coef[4:5] = weight
-
-    @pl.when(gx == 0)
-    def _():
-        ext[:, 0:SIDE, LANES:LANES + ny] = jnp.zeros((2 * comps, SIDE, ny), jnp.bfloat16)
-
-    @pl.when(gx == gxs - 1)
-    def _():
-        ext[:, SIDE + nx:, LANES:LANES + ny] = jnp.zeros((2 * comps, SIDE, ny), jnp.bfloat16)
-
-    @pl.when(gy == 0)
-    def _():
-        for p in range(2 * comps):
-            ext[p, SIDE:SIDE + nx, 0:LANES] = jnp.zeros((nx, LANES), jnp.bfloat16)
-
-    @pl.when(gy == 1)
-    def _():
-        for p in range(2 * comps):
-            ext[p, SIDE:SIDE + nx, LANES + ny:] = jnp.zeros((nx, LANES), jnp.bfloat16)
-
     below = (gx + gxs - 1) // gxs
     above = (2 * gxs - 2 - gx) // gxs
     pl.semaphore_wait(barrier, bands + below + above)
@@ -174,6 +143,37 @@
         return carry
 
     lax.fori_loop(0, pieces, start_y, 0)
+    along_a[...] = band_matrix((ROWS, ROWS + 2 * SIDE), SIDE, False)
+    along_b[...] = band_matrix((half + 2 * LANES, half), LANES, True)
+    freq = jnp.full((1, ny), freq_ref[0], jnp.int32).astype(jnp.float32)
+    span = jnp.full((1, ny), span_ref[0], jnp.int32).astype(jnp.float32)
+    omega = (freq + 1.0) / FREQS
+    beta = (span - (SPANS - 1) / 2.0) * 2.0 / SPANS
+    weight = 1.0 / (0.5 + omega)
+    coef[0:1] = weight / 12.0
+    coef[1:2] = weight / 12.0
+    coef[2:3] = -beta * weight
+    coef[3:4] = omega * weight
+    coef[4:5] = weight
+
+    @pl.when(gx == 0)
+    def _():
+        ext[:, 0:SIDE, LANES:LANES + ny] = jnp.zeros((2 * comps, SIDE, ny), jnp.bfloat16)
+
+    @pl.when(gx == gxs - 1)
+    def _():
+        ext[:, SIDE + nx:, LANES:LANES + ny] = jnp.zeros((2 * comps, SIDE, ny), jnp.bfloat16)
+
+    @pl.when(gy == 0)
+    def _():
+        for p in range(2 * comps):
+            ext[p, SIDE:SIDE + nx, 0:LANES] = jnp.zeros((nx, LANES), jnp.bfloat16)
+
+    @pl.when(gy == 1)
+    def _():
+        for p in range(2 * comps):
+            ext[p, SIDE:SIDE + nx, LANES + ny:] = jnp.zeros((nx, LANES), jnp.bfloat16)
+
     for edge in range(bands + 1):
         joint_copy(edge).wait()
     strip_copy(3).wait()
@@ -367,8 +367,8 @@
     anywhere = pl.BlockSpec(memory_space=pl.ANY)
     scalar = pl.BlockSpec(memory_space=pltpu.SMEM)
     dma = pltpu.SemaphoreType.DMA
-    return pl.pallas_call(
-        functools.partial(kernel, bands, gxs, comps, pieces, forward.shape[0] * bands),
+    total = pl.pallas_call(
+        functools.partial(kernel, bands, gxs, comps, pieces),
         out_shape=jax.ShapeDtypeStruct((5, nx // bands, ny), jnp.float32),
         in_specs=[scalar, scalar, anywhere, anywhere],
         out_specs=anywhere,
@@ -400,6 +400,7 @@
         freq_index, span_index,
         forward.reshape(planes, nx, ny), adjoint.reshape(planes, nx, ny),
     )
+    return total * (1.0 / math.sqrt(comps * bands * forward.shape[0]))
 
 
 def solution(mesh):

time: 60 us -> 59.9 us (level)
  local copies, waits for them, and re-layouts: 3.62 us -> 0 us
  other arithmetic: 0 us -> 3.6 us
    unnamed x1 -> x0, local copies, waits for them, and re-layouts: 3.62 us -> none
    mul x0 -> x1, other arithmetic: none -> 3.6 us  [local(): return total * (1.0 / math.sqrt(comps * bands * forward.shape[0]))]
where the time goes in v3:
time: 59.9 us; the launch traced here: 59.8 us
  Pallas kernels  54.9 us (92%)
  other arithmetic  3.6 us (6%)
  between operations  1.3 us (2%)
    pallas_call x1, Pallas kernels, local(): pl.pallas_call(functools.partial(kernel, bands, gxs, comps, pieces), out_...  54.9 us
    mul x1, other arithmetic, local(): return total * (1.0 / math.sqrt(comps * bands * forward.shape[0]))  3.6 us

profile of v3, /device:TPU:0, one launch (start us, length us, event | category | flops | bytes accessed | tf_op | source)
XLA Modules:
  0.0 59.8 jit_solution(8376388568563903714)
XLA Ops:
  1.3 54.9 %shard_map.46 = f32[5,256,512]{2,1,0:T(8,128)} custom-call(s32[1]{0:T(128)S(6)} %copy.5.freq_ref, s32[1]{0:T(128)S(6)} %copy.6.span_ref, bf16[10,1024,512]{2,1,0:T(8,128)(2,1)} %bitcast.2, bf16[10,1024,512]{2,1,0:T(8,128)(2,1)} %bitcast.3), custom_call_target="tpu_custom_call" | custom-call | flops 104857600 | bytes 20971520 | tf_op jit(solution)/shard_map/pallas_call | solution.py:370
  56.2 3.6 %broadcast_multiply_fusion = f32[5,256,512]{2,1,0:T(8,128)} fusion(f32[5,256,512]{2,1,0:T(8,128)} %shard_map.46), kind=kLoop, calls=%fused_computation | loop fusion | flops 655360 | bytes 5242880 | tf_op jit(solution)/shard_map/mul | solution.py:403
